TPU v7x, 32 devices: a whole 2x2x4 slice. The times are simulated.
32 devices in a mesh: pop: 8 (over z, x), tensor: 4 (over y, core).
Axes of the slice: x: 2, y: 2, z: 4, core: 2. Of those that a mesh axis runs over, the one named last changes fastest.
Arguments:
- token_ids: int32 [64, 64], P('pop'), may hold values from 0 to 76031, as said below
- ranks: int32 [64], P('pop'), may hold values from 0 to 63, each once
- embed_table: bfloat16 [76032, 3584], P('pop', 'tensor'), may hold values from -6 to 6
- norm_gain: bfloat16 [3584], replicated, may hold values from 0.5 to 1.5
- gate_weight: bfloat16 [3584, 18944], P('pop', 'tensor'), may hold values from -0.09375 to 0.09375
- up_weight: bfloat16 [3584, 18944], P('pop', 'tensor'), may hold values from -0.09375 to 0.09375
- gate_left: bfloat16 [64, 3584], P('pop'), may hold values from -6 to 6
- up_left: bfloat16 [64, 3584], P('pop'), may hold values from -6 to 6
- gate_right: bfloat16 [64, 18944], P('pop', 'tensor'), may hold values from -6 to 6
- up_right: bfloat16 [64, 18944], P('pop', 'tensor'), may hold values from -6 to 6
Outputs:
- hidden: bfloat16 [4096, 18944], P('pop', 'tensor')
- gate_step: float32 [3584, 18944], P('pop', 'tensor')
- up_step: float32 [3584, 18944], P('pop', 'tensor')
Inputs may be any that keep to these rules, and one draw needn't show every extreme that they name: Split token_ids into aligned blocks of 8 members (the members of one index of pop) and the table into blocks of 9504 rows: in every block of members, at most 128 ids fall in any one block of table rows, and exactly 128 in one of them.
All inputs are finite; a program needn't handle non-finite values.
Results may differ from a plain program's by a relative error of at most 0.0058.
Values may be sent and summed in bfloat16 or wider, within the bound.
A program may use at most 256 MiB of HBM per device.

v0:
```python
import math
import jax
import jax.numpy as jnp
from jax import lax
from jax.sharding import PartitionSpec as P


def split_high(x):
    high = lax.reduce_precision(x, exponent_bits=8, mantissa_bits=7)
    low = x - high
    return jnp.concatenate([high.astype(jnp.bfloat16), low.astype(jnp.bfloat16)], axis=0)


def weighted_step(left, right, score):
    scaled = split_high(left.astype(jnp.float32) * score[:, None])
    both = jnp.concatenate([right, right], axis=0)
    return lax.dot_general(
        scaled, both, (((0,), (0,)), ((), ())), preferred_element_type=jnp.float32
    )


def per_device(
    token_ids,
    ranks,
    embed_table,
    norm_gain,
    gate_weight,
    up_weight,
    gate_left,
    up_left,
    gate_right,
    up_right,
):
    pops = lax.axis_size("pop")
    pop = lax.axis_index("pop")
    tensor = lax.axis_index("tensor")
    table_rows, features = embed_table.shape
    own_members, prompt = token_ids.shape
    row_count, hidden_cols = gate_weight.shape
    width = norm_gain.shape[0]
    members = own_members * pops
    part = -(-hidden_cols // (128 * pops)) * 128
    padded = part * pops

    def pad_cols(x):
        return jnp.pad(x, ((0, 0), (0, padded - hidden_cols)))

    all_ids = lax.all_gather(token_ids, "pop", axis=0, tiled=True)
    all_ranks = lax.all_gather(ranks, "pop", axis=0, tiled=True)
    local_ids = all_ids.reshape(-1) - pop * table_rows
    owned = (local_ids >= 0) & (local_ids < table_rows)
    picked = jnp.take(embed_table, jnp.clip(local_ids, 0, table_rows - 1), axis=0)
    partial_rows = jnp.where(owned[:, None], picked, jnp.bfloat16(0))
    own_cols = lax.psum_scatter(partial_rows, "pop", scatter_dimension=0, tiled=True)
    gate_cols = lax.all_to_all(pad_cols(gate_weight), "pop", 1, 0, tiled=True)
    up_cols = lax.all_to_all(pad_cols(up_weight), "pop", 1, 0, tiled=True)
    values = own_cols.astype(jnp.float32)
    total = lax.psum(jnp.sum(values * values, axis=-1), "tensor")
    gain = lax.dynamic_slice_in_dim(norm_gain, tensor * features, features, 0)
    own_normed = (
        values * lax.rsqrt(total[:, None] * (1.0 / width) + 1e-06) * gain.astype(jnp.float32)
    ).astype(jnp.bfloat16)
    some = lax.all_gather(own_normed, "pop", axis=0, tiled=True)
    normed = lax.all_gather(some, "tensor", axis=1, tiled=True)
    all_gl, all_ul, all_gr, all_ur = (
        lax.all_gather(gate_left, "pop", axis=0, tiled=True),
        lax.all_gather(up_left, "pop", axis=0, tiled=True),
        lax.all_gather(gate_right, "pop", axis=0, tiled=True),
        lax.all_gather(up_right, "pop", axis=0, tiled=True),
    )
    scale = 0.5 / math.sqrt(width)
    blocks = normed.reshape(members, prompt, width)

    def project(weight, left, right):
        base = jnp.dot(normed, weight, preferred_element_type=jnp.float32)
        side = jnp.einsum("mld,md->ml", blocks, left, preferred_element_type=jnp.float32) * scale
        cols = lax.dynamic_slice_in_dim(pad_cols(right), pop * part, part, 1)
        return (
            base.reshape(members, prompt, part)
            + side[:, :, None] * cols.astype(jnp.float32)[:, None, :]
        )

    gate = project(gate_cols, all_gl, all_gr)
    up = project(up_cols, all_ul, all_ur)
    mine = (jax.nn.silu(gate) * up).astype(jnp.bfloat16).reshape(members * prompt, part)
    hidden = lax.all_to_all(mine, "pop", 0, 1, tiled=True)[:, :hidden_cols]
    score = (2.0 * all_ranks.astype(jnp.float32) - (members - 1)) / (members - 1)
    score = score * (1.0 / math.sqrt(members))
    row_start = pop * row_count
    left_gate = lax.dynamic_slice_in_dim(all_gl, row_start, row_count, 1)
    left_up = lax.dynamic_slice_in_dim(all_ul, row_start, row_count, 1)
    gate_step = weighted_step(left_gate, all_gr, score)
    up_step = weighted_step(left_up, all_ur, score)
    return (hidden, gate_step, up_step)


def solution(mesh):
    in_specs = (
        P("pop", None),
        P("pop"),
        P("pop", "tensor"),
        P(),
        P("pop", "tensor"),
        P("pop", "tensor"),
        P("pop", None),
        P("pop", None),
        P("pop", "tensor"),
        P("pop", "tensor"),
    )
    out_specs = (P("pop", "tensor"), P("pop", "tensor"), P("pop", "tensor"))
    return jax.shard_map(
        per_device, mesh=mesh, in_specs=in_specs, out_specs=out_specs, check_vma=False
    )
```

profile of v0, /device:TPU:0, one launch (start us, length us, event | category | flops | bytes accessed | tf_op | source)
XLA Modules:
  0.0 799.4 jit_solution(13260142982139188664)
XLA Ops:
  7.2 32.3 %all_gather.24 = s32[64,64]{1,0:T(8,128)S(1)} all-gather(s32[8,64]{1,0:T(8,128)} %param.10), channel_id=1, replica_groups=mesh['pop'=8,'tensor'=4] {'pop'}, dimensions={0}, use_global_device_ids=true | all-gather | bytes 18432 | tf_op jit(solution)/shard_map/all_gather | solution.py:48
  39.9 27.8 %gather_fusion = bf16[4096,896]{1,0:T(8,128)(2,1)} fusion(bf16[9504,896]{1,0:T(8,128)(2,1)} %param.12, s32[4096]{0:T(1024)S(1)} %broadcast_clamp_fusion), kind=kCustom, calls=%fused_computation | custom fusion | bytes 14696448 | tf_op jit(solution)/shard_map/jit(_take)/gather | solution.py:52
  67.7 7.0 select_select_fusion
  75.5 132.9 %reduce-scatter.2.cloned.1.call-done = bf16[512,896]{1,0:T(8,128)(2,1)} async-done(((bf16[4096,896]{1,0:T(8,128)(2,1)}), bf16[512,896]{1,0:T(8,128)(2,1)}) %reduce-scatter.2.cloned.1.call-update) | async-done | bytes 917520 | tf_op jit(solution)/shard_map/reduce_scatter | solution.py:54
  209.9 5.7 psum.7
  218.0 111.5 %all-gather.3.cloned.1.call-done = bf16[4096,896]{1,0:T(8,128)(2,1)} async-done(((bf16[512,896]{1,0:T(8,128)(2,1)}), bf16[4096,896]{1,0:T(8,128)(2,1)}) %all-gather.3.cloned.1.call-update) | async-done | bytes 7340048 | tf_op jit(solution)/shard_map/all_gather | solution.py:63
  334.9 4.8 all-to-all-start
  339.7 4.0 pad.16
  343.7 3.2 copy.29
  346.9 115.7 %all_gather.28 = bf16[64,4736]{1,0:T(8,128)(2,1)S(1)} all-gather(bf16[8,4736]{1,0:T(8,128)(2,1)S(1)} %copy-done), channel_id=1, replica_groups=mesh['pop'=8,'tensor'=4] {'pop'}, dimensions={0}, use_global_device_ids=true | all-gather | bytes 681984 | tf_op jit(solution)/shard_map/all_gather | solution.py:68
  462.7 31.8 %all_gather.30 = bf16[64,4736]{1,0:T(8,128)(2,1)S(1)} all-gather(bf16[8,4736]{1,0:T(8,128)(2,1)S(1)} %copy-done.1), channel_id=1, replica_groups=mesh['pop'=8,'tensor'=4] {'pop'}, dimensions={0}, use_global_device_ids=true | all-gather | bytes 681984 | tf_op jit(solution)/shard_map/all_gather | solution.py:69
  494.5 31.3 %all_gather.27 = bf16[64,3584]{1,0:T(8,128)(2,1)S(1)} all-gather(bf16[8,3584]{1,0:T(8,128)(2,1)S(1)} %copy-done.2), channel_id=1, replica_groups=mesh['pop'=8,'tensor'=4] {'pop'}, dimensions={0}, use_global_device_ids=true | all-gather | bytes 516096 | tf_op jit(solution)/shard_map/all_gather | solution.py:66
  525.8 40.9 %all_gather.29 = bf16[64,3584]{1,0:T(8,128)(2,1)S(1)} all-gather(bf16[8,3584]{1,0:T(8,128)(2,1)S(1)} %copy-done.3), channel_id=1, replica_groups=mesh['pop'=8,'tensor'=4] {'pop'}, dimensions={0}, use_global_device_ids=true | all-gather | bytes 516096 | tf_op jit(solution)/shard_map/all_gather | solution.py:67
  566.7 15.6 %all-to-all-start.1 = ((bf16[448,8,640]{2,0,1:T(8,128)(2,1)}), bf16[448,8,640]{2,0,1:T(8,128)(2,1)}, u32[]{:S(2)}, u32[]{:S(2)}) async-start(bf16[448,8,640]{2,0,1:T(8,128)(2,1)} %bitcast.38), calls=%async_computation.2 | async-start | bytes 9175040 | tf_op jit(solution)/shard_map/all_to_all | solution.py:56
  582.3 13.1 %fusion.11 = f32[64,1,64]{2,1,0:T(1,128)S(1)} fusion(bf16[64,64,3584]{2,1,0:T(8,128)(2,1)} %bitcast.48, bf16[64,3584,1]{1,0,2:T(8,128)(2,1)S(1)} %bitcast.44), kind=kOutput, calls=%fused_computation.18 | convolution fusion | flops 29360128 | bytes 29835264 | tf_op jit(solution)/shard_map/mld,md->ml/dot_general | solution.py:76
  595.4 13.1 %fusion.13 = f32[64,1,64]{2,1,0:T(1,128)S(1)} fusion(bf16[64,64,3584]{2,1,0:T(8,128)(2,1)} %bitcast.49, bf16[64,3584,1]{1,0,2:T(8,128)(2,1)S(1)} %bitcast.43), kind=kOutput, calls=%fused_computation.20 | convolution fusion | flops 29360128 | bytes 29835264 | tf_op jit(solution)/shard_map/mld,md->ml/dot_general | solution.py:76
  608.4 29.4 %fusion.27 = f32[64,64,640]{2,1,0:T(8,128)} fusion(bf16[64,64,3584]{2,1,0:T(8,128)(2,1)} %bitcast.50, bf16[3584,640,1]{1,0,2:T(8,128)(2,1)} %bitcast.4), kind=kOutput, calls=%fused_computation.53 | convolution fusion | flops 18790481920 | bytes 44433408 | tf_op jit(solution)/shard_map/dot_general | solution.py:75
  637.8 5.0 all-to-all-done.1
  642.8 30.8 %multiply_convert_fusion = bf16[64,64,640]{2,1,0:T(8,128)(2,1)} fusion(f32[64,64,640]{2,1,0:T(8,128)} %fusion.27, f32[64,640]{1,0:T(8,128)S(1)} %fusion.24, f32[64,64]{1,0:T(8,128)S(1)} %get-tuple-element.9, f32[64,640]{1,0:T(8,128)S(1)} %fusion.23, f32[64,64]{1,0:T(8,128)S(1)} %get-tuple-element.10, bf16[64,64,3584]{2,1,0:T(8,128)(2,1)} %bitcast.51, ...), kind=kOutput, calls=%fused_computation.1 | convolution fusion | flops 18816696320 | bytes 50036736 | tf_op jit(solution)/shard_map/dot_general | solution.py:75
  673.6 4.8 all-to-all-start.2
  679.9 97.4 %all-reduce.4 = s32[64]{0:T(128)S(1)} all-reduce(s32[64]{0:T(128)S(1)} %dynamic-update-slice), channel_id=1, replica_groups=mesh['pop'=8,'tensor'=4] {'pop'}, use_global_device_ids=true, to_apply=%add.4 | all-reduce | flops 64 | bytes 512
  777.5 4.7 fusion.7
  782.2 4.7 fusion.3
  786.9 3.3 copy.22
  (44 shorter events, 14.1 us)
Async XLA Ops:
  7.2 201.3 %reduce-scatter.2.cloned.1.call-start = ((), (), s32[]{:S(2)}) async-start(), calls=%async_computation.4 | async-start | bytes 8257536 | tf_op jit(solution)/shard_map/reduce_scatter | solution.py:54
  74.7 254.8 %all-gather.3.cloned.1.call-start = ((), (), s32[]{:S(2)}) async-start(), calls=%async_computation.5 | async-start | bytes 8257536 | tf_op jit(solution)/shard_map/all_gather | solution.py:63
  218.0 364.3 %all-gather.5.cloned.1.call-start = ((), (), s32[]{:S(2)}) async-start(), calls=%async_computation.6 | async-start | bytes 36700160 | tf_op jit(solution)/shard_map/all_gather | solution.py:64
  334.9 231.8 %all-to-all-start = ((bf16[448,8,640]{2,0,1:T(8,128)(2,1)}), bf16[448,8,640]{2,0,1:T(8,128)(2,1)}, u32[]{:S(2)}, u32[]{:S(2)}) async-start(bf16[448,8,640]{2,0,1:T(8,128)(2,1)} %bitcast.39), calls=%async_computation.1 | async-start | bytes 9175040 | tf_op jit(solution)/shard_map/all_to_all | solution.py:55
  339.7 7.2 copy-start
  343.7 119.0 %copy-start.1 = (bf16[8,4736]{1,0:T(8,128)(2,1)S(1)}, bf16[8,4736]{1,0:T(8,128)(2,1)}, u32[]{:S(2)}) copy-start(bf16[8,4736]{1,0:T(8,128)(2,1)} %param.19) | copy-start | bytes 227332
  343.7 150.8 %copy-start.2 = (bf16[8,3584]{1,0:T(8,128)(2,1)S(1)}, bf16[8,3584]{1,0:T(8,128)(2,1)}, u32[]{:S(2)}) copy-start(bf16[8,3584]{1,0:T(8,128)(2,1)} %param.16) | copy-start | bytes 172036
  343.7 182.1 %copy-start.3 = (bf16[8,3584]{1,0:T(8,128)(2,1)S(1)}, bf16[8,3584]{1,0:T(8,128)(2,1)}, u32[]{:S(2)}) copy-start(bf16[8,3584]{1,0:T(8,128)(2,1)} %param.17) | copy-start | bytes 172036
  566.7 76.1 %all-to-all-start.1 = ((bf16[448,8,640]{2,0,1:T(8,128)(2,1)}), bf16[448,8,640]{2,0,1:T(8,128)(2,1)}, u32[]{:S(2)}, u32[]{:S(2)}) async-start(bf16[448,8,640]{2,0,1:T(8,128)(2,1)} %bitcast.38), calls=%async_computation.2 | async-start | bytes 9175040 | tf_op jit(solution)/shard_map/all_to_all | solution.py:56
  673.6 4.8 copy-start.5
  673.6 6.1 copy-start.4
  673.6 113.3 %all-to-all-start.2 = ((bf16[8,512,640]{2,1,0:T(8,128)(2,1)}), bf16[8,512,640]{2,1,0:T(8,128)(2,1)}, u32[]{:S(2)}, u32[]{:S(2)}) async-start(bf16[8,512,640]{2,1,0:T(8,128)(2,1)} %bitcast.42), calls=%async_computation.3 | async-start | bytes 10485760 | tf_op jit(solution)/shard_map/all_to_all | solution.py:86
Sparse Core Ops, SparseCore 0:
  74.8 133.5 reduce-scatter.1
  218.1 111.3 all-gather.2
  331.1 175.9 all-gather.4
where the time goes:
time: 800 us; the launch traced here: 799 us
  blocking collectives  355 us (44%)
  waiting for transfers between devices  249 us (31%)
  matrix products  95.7 us (12%)
  local copies, waits for them, and re-layouts  47.3 us (6%)
  starting transfers between devices  25.3 us (3%)
  between operations  14.6 us (2%)
  other arithmetic  11.9 us (1%)
    reduce_scatter x1, waiting for transfers between devices, per_device(): lax.psum_scatter(partial_rows, 'pop', scatter_dimension=0, tiled=True)  133 us
    all_gather x1, blocking collectives, per_device(): lax.all_gather(gate_right, 'pop', axis=0, tiled=True)  116 us
    all_gather x1, waiting for transfers between devices, per_device(): some = lax.all_gather(own_normed, 'pop', axis=0, tiled=True)  111 us
    unnamed x1, blocking collectives  97.4 us
    dot_general x2, matrix products, project(): base = jnp.dot(normed, weight, preferred_element_type=jnp.float32)  60.2 us
    all_gather x1, blocking collectives, per_device(): lax.all_gather(up_left, 'pop', axis=0, tiled=True)  40.9 us
    all_gather x1, blocking collectives, per_device(): all_ids = lax.all_gather(token_ids, 'pop', axis=0, tiled=True)  32.3 us
    all_gather x1, blocking collectives, per_device(): lax.all_gather(up_right, 'pop', axis=0, tiled=True)  31.8 us
  transfers between devices with their start and end apart: 6, of which 3 were waited for; matrix products, arithmetic and copies ran while one was open for 10% of the time, Pallas kernels for 0%

commit v1 on v0

--- a/solution.py
+++ b/solution.py
@@ -45,7 +45,12 @@
     def pad_cols(x):
         return jnp.pad(x, ((0, 0), (0, padded - hidden_cols)))
 
-    all_ids = lax.all_gather(token_ids, "pop", axis=0, tiled=True)
+    ring = [token_ids]
+    for hop in range(7):
+        ring.append(lax.ppermute(ring[-1], "pop", [(dev, (dev + 1) % 8) for dev in range(8)]))
+    all_ids = jnp.roll(
+        jnp.concatenate(ring[::-1], axis=0), (lax.axis_index("pop") + 1) * ring[0].shape[0], axis=0
+    )
     all_ranks = lax.all_gather(ranks, "pop", axis=0, tiled=True)
     local_ids = all_ids.reshape(-1) - pop * table_rows
     owned = (local_ids >= 0) & (local_ids < table_rows)

time: 800 us -> 812 us (1.015)
  waiting for transfers between devices: 249 us -> 289 us
  blocking collectives: 355 us -> 323 us
    ppermute x0 -> x7, waiting for transfers between devices: none -> 42.6 us  [per_device(): lax.ppermute(ring[-1], 'pop', [(dev, (dev + 1) % 8) for dev in range(8)])]
    all_gather x1 -> x0, blocking collectives: 32.3 us -> none  [per_device(): all_ids = lax.all_gather(token_ids, 'pop', axis=0, tiled=True)]
  transfers between devices with their start and end apart: 6 -> 13, of which waited for: 3 -> 10; matrix products, arithmetic and copies ran while one was open for 10% -> 10% of each run, Pallas kernels for 0% -> 0%
where the time goes in v1:
time: 812 us; the launch traced here: 811 us
  blocking collectives  323 us (40%)
  waiting for transfers between devices  289 us (36%)
  matrix products  95.7 us (12%)
  local copies, waits for them, and re-layouts  48.7 us (6%)
  starting transfers between devices  28.3 us (3%)
  between operations  14.7 us (2%)
  other arithmetic  11.9 us (1%)
    reduce_scatter x1, waiting for transfers between devices, per_device(): lax.psum_scatter(partial_rows, 'pop', scatter_dimension=0, tiled=True)  129 us
    all_gather x1, blocking collectives, per_device(): lax.all_gather(gate_right, 'pop', axis=0, tiled=True)  116 us
    all_gather x1, waiting for transfers between devices, per_device(): some = lax.all_gather(own_normed, 'pop', axis=0, tiled=True)  111 us
    unnamed x1, blocking collectives  97.4 us
    dot_general x2, matrix products, project(): base = jnp.dot(normed, weight, preferred_element_type=jnp.float32)  60.1 us
    ppermute x7, waiting for transfers between devices, per_device(): lax.ppermute(ring[-1], 'pop', [(dev, (dev + 1) % 8) for dev in range(8)])  42.6 us
    all_gather x1, blocking collectives, per_device(): lax.all_gather(up_left, 'pop', axis=0, tiled=True)  40.9 us
    all_gather x1, blocking collectives, per_device(): lax.all_gather(up_right, 'pop', axis=0, tiled=True)  31.8 us
  transfers between devices with their start and end apart: 13, of which 10 were waited for; matrix products, arithmetic and copies ran while one was open for 10% of the time, Pallas kernels for 0%

profile of v1, /device:TPU:0, one launch (start us, length us, event | category | flops | bytes accessed | tf_op | source)
XLA Modules:
  0.0 810.7 jit_solution(15911301314163899613)
XLA Ops:
  10.2 4.8 collective-permute-done
  15.0 6.3 collective-permute-done.1
  21.3 6.3 collective-permute-done.2
  27.7 6.3 collective-permute-done.3
  34.0 6.3 collective-permute-done.4
  40.3 6.3 collective-permute-done.5
  46.6 6.3 collective-permute-done.6
  54.7 27.8 %gather_fusion = bf16[4096,896]{1,0:T(8,128)(2,1)} fusion(bf16[9504,896]{1,0:T(8,128)(2,1)} %param.12, s32[4096]{0:T(1024)S(1)} %broadcast_clamp_fusion), kind=kCustom, calls=%fused_computation | custom fusion | bytes 14696448 | tf_op jit(solution)/shard_map/jit(_take)/gather | solution.py:57
  82.4 7.0 select_select_fusion
  90.3 129.5 %reduce-scatter.2.cloned.1.call-done = bf16[512,896]{1,0:T(8,128)(2,1)} async-done(((bf16[4096,896]{1,0:T(8,128)(2,1)}), bf16[512,896]{1,0:T(8,128)(2,1)}) %reduce-scatter.2.cloned.1.call-update) | async-done | bytes 917520 | tf_op jit(solution)/shard_map/reduce_scatter | solution.py:59
  221.3 5.7 psum.7
  229.4 111.5 %all-gather.3.cloned.1.call-done = bf16[4096,896]{1,0:T(8,128)(2,1)} async-done(((bf16[512,896]{1,0:T(8,128)(2,1)}), bf16[4096,896]{1,0:T(8,128)(2,1)}) %all-gather.3.cloned.1.call-update) | async-done | bytes 7340048 | tf_op jit(solution)/shard_map/all_gather | solution.py:68
  358.3 115.7 %all_gather.24 = bf16[64,4736]{1,0:T(8,128)(2,1)S(1)} all-gather(bf16[8,4736]{1,0:T(8,128)(2,1)S(1)} %copy-done), channel_id=1, replica_groups=mesh['pop'=8,'tensor'=4] {'pop'}, dimensions={0}, use_global_device_ids=true | all-gather | bytes 681984 | tf_op jit(solution)/shard_map/all_gather | solution.py:73
  474.0 31.8 %all_gather.26 = bf16[64,4736]{1,0:T(8,128)(2,1)S(1)} all-gather(bf16[8,4736]{1,0:T(8,128)(2,1)S(1)} %copy-done.1), channel_id=1, replica_groups=mesh['pop'=8,'tensor'=4] {'pop'}, dimensions={0}, use_global_device_ids=true | all-gather | bytes 681984 | tf_op jit(solution)/shard_map/all_gather | solution.py:74
  505.9 31.3 %all_gather.23 = bf16[64,3584]{1,0:T(8,128)(2,1)S(1)} all-gather(bf16[8,3584]{1,0:T(8,128)(2,1)S(1)} %copy-done.2), channel_id=1, replica_groups=mesh['pop'=8,'tensor'=4] {'pop'}, dimensions={0}, use_global_device_ids=true | all-gather | bytes 516096 | tf_op jit(solution)/shard_map/all_gather | solution.py:71
  537.1 40.9 %all_gather.25 = bf16[64,3584]{1,0:T(8,128)(2,1)S(1)} all-gather(bf16[8,3584]{1,0:T(8,128)(2,1)S(1)} %copy-done.3), channel_id=1, replica_groups=mesh['pop'=8,'tensor'=4] {'pop'}, dimensions={0}, use_global_device_ids=true | all-gather | bytes 516096 | tf_op jit(solution)/shard_map/all_gather | solution.py:72
  578.0 15.6 %all-to-all-start.1 = ((bf16[448,8,640]{2,0,1:T(8,128)(2,1)}), bf16[448,8,640]{2,0,1:T(8,128)(2,1)}, u32[]{:S(2)}, u32[]{:S(2)}) async-start(bf16[448,8,640]{2,0,1:T(8,128)(2,1)} %bitcast.38), calls=%async_computation.2 | async-start | bytes 9175040 | tf_op jit(solution)/shard_map/all_to_all | solution.py:61
  593.7 13.1 %fusion.11 = f32[64,1,64]{2,1,0:T(1,128)S(1)} fusion(bf16[64,64,3584]{2,1,0:T(8,128)(2,1)} %bitcast.48, bf16[64,3584,1]{1,0,2:T(8,128)(2,1)S(1)} %bitcast.44), kind=kOutput, calls=%fused_computation.18 | convolution fusion | flops 29360128 | bytes 29835264 | tf_op jit(solution)/shard_map/mld,md->ml/dot_general | solution.py:81
  606.7 13.1 %fusion.13 = f32[64,1,64]{2,1,0:T(1,128)S(1)} fusion(bf16[64,64,3584]{2,1,0:T(8,128)(2,1)} %bitcast.49, bf16[64,3584,1]{1,0,2:T(8,128)(2,1)S(1)} %bitcast.43), kind=kOutput, calls=%fused_computation.20 | convolution fusion | flops 29360128 | bytes 29835264 | tf_op jit(solution)/shard_map/mld,md->ml/dot_general | solution.py:81
  619.8 29.4 %fusion.28 = f32[64,64,640]{2,1,0:T(8,128)} fusion(bf16[64,64,3584]{2,1,0:T(8,128)(2,1)} %bitcast.50, bf16[3584,640,1]{1,0,2:T(8,128)(2,1)} %bitcast.4), kind=kOutput, calls=%fused_computation.70 | convolution fusion | flops 18790481920 | bytes 44433408 | tf_op jit(solution)/shard_map/dot_general | solution.py:80
  649.1 5.0 all-to-all-done.1
  654.1 30.8 %multiply_convert_fusion = bf16[64,64,640]{2,1,0:T(8,128)(2,1)} fusion(f32[64,64,640]{2,1,0:T(8,128)} %fusion.28, f32[64,640]{1,0:T(8,128)S(1)} %fusion.24, f32[64,64]{1,0:T(8,128)S(1)} %get-tuple-element.9, f32[64,640]{1,0:T(8,128)S(1)} %fusion.23, f32[64,64]{1,0:T(8,128)S(1)} %get-tuple-element.10, bf16[64,64,3584]{2,1,0:T(8,128)(2,1)} %bitcast.51, ...), kind=kOutput, calls=%fused_computation.1 | convolution fusion | flops 18816696320 | bytes 50036736 | tf_op jit(solution)/shard_map/dot_general | solution.py:80
  684.9 4.8 all-to-all-start.2
  691.2 97.4 %all-reduce.4 = s32[64]{0:T(128)S(1)} all-reduce(s32[64]{0:T(128)S(1)} %dynamic-update-slice), channel_id=1, replica_groups=mesh['pop'=8,'tensor'=4] {'pop'}, use_global_device_ids=true, to_apply=%add.4 | all-reduce | flops 64 | bytes 512
  (73 shorter events, 43.2 us)
Async XLA Ops:
  7.2 212.7 %reduce-scatter.2.cloned.1.call-start = ((), (), s32[]{:S(2)}) async-start(), calls=%async_computation.4 | async-start | bytes 8257536 | tf_op jit(solution)/shard_map/reduce_scatter | solution.py:59
  7.2 7.8 collective-permute-start
  15.0 6.3 collective-permute-start.1
  21.3 6.3 collective-permute-start.2
  27.6 6.3 collective-permute-start.3
  34.0 6.3 collective-permute-start.4
  40.3 6.3 collective-permute-start.5
  46.6 6.3 collective-permute-start.6
  89.5 251.3 %all-gather.3.cloned.1.call-start = ((), (), s32[]{:S(2)}) async-start(), calls=%async_computation.5 | async-start | bytes 8257536 | tf_op jit(solution)/shard_map/all_gather | solution.py:68
  229.3 364.3 %all-gather.5.cloned.1.call-start = ((), (), s32[]{:S(2)}) async-start(), calls=%async_computation.6 | async-start | bytes 36700160 | tf_op jit(solution)/shard_map/all_gather | solution.py:69
  346.3 231.8 %all-to-all-start = ((bf16[448,8,640]{2,0,1:T(8,128)(2,1)}), bf16[448,8,640]{2,0,1:T(8,128)(2,1)}, u32[]{:S(2)}, u32[]{:S(2)}) async-start(bf16[448,8,640]{2,0,1:T(8,128)(2,1)} %bitcast.39), calls=%async_computation.1 | async-start | bytes 9175040 | tf_op jit(solution)/shard_map/all_to_all | solution.py:60
  351.1 7.2 copy-start
  355.0 119.0 %copy-start.1 = (bf16[8,4736]{1,0:T(8,128)(2,1)S(1)}, bf16[8,4736]{1,0:T(8,128)(2,1)}, u32[]{:S(2)}) copy-start(bf16[8,4736]{1,0:T(8,128)(2,1)} %param.19) | copy-start | bytes 227332
  355.1 150.8 %copy-start.2 = (bf16[8,3584]{1,0:T(8,128)(2,1)S(1)}, bf16[8,3584]{1,0:T(8,128)(2,1)}, u32[]{:S(2)}) copy-start(bf16[8,3584]{1,0:T(8,128)(2,1)} %param.16) | copy-start | bytes 172036
  355.1 182.1 %copy-start.3 = (bf16[8,3584]{1,0:T(8,128)(2,1)S(1)}, bf16[8,3584]{1,0:T(8,128)(2,1)}, u32[]{:S(2)}) copy-start(bf16[8,3584]{1,0:T(8,128)(2,1)} %param.17) | copy-start | bytes 172036
  578.0 76.1 %all-to-all-start.1 = ((bf16[448,8,640]{2,0,1:T(8,128)(2,1)}), bf16[448,8,640]{2,0,1:T(8,128)(2,1)}, u32[]{:S(2)}, u32[]{:S(2)}) async-start(bf16[448,8,640]{2,0,1:T(8,128)(2,1)} %bitcast.38), calls=%async_computation.2 | async-start | bytes 9175040 | tf_op jit(solution)/shard_map/all_to_all | solution.py:61
  684.9 4.8 copy-start.5
  684.9 6.1 copy-start.4
  684.9 113.3 %all-to-all-start.2 = ((bf16[8,512,640]{2,1,0:T(8,128)(2,1)}), bf16[8,512,640]{2,1,0:T(8,128)(2,1)}, u32[]{:S(2)}, u32[]{:S(2)}) async-start(bf16[8,512,640]{2,1,0:T(8,128)(2,1)} %bitcast.42), calls=%async_computation.3 | async-start | bytes 10485760 | tf_op jit(solution)/shard_map/all_to_all | solution.py:91
Sparse Core Ops, SparseCore 0:
  89.6 130.1 reduce-scatter.1
  229.5 111.3 all-gather.2
  342.4 175.9 all-gather.4
